TPU v7x, 256 devices: a whole 4x4x8 slice. The times are simulated.
256 devices in a mesh: ctx: 32 (over z, x_hi, core), head: 8 (over y, x_lo).
Axes of the slice: x: 4 (x_hi: 2, x_lo: 2; x = x_hi * 2 + x_lo), y: 4, z: 8, core: 2. Of those that a mesh axis runs over, the one named last changes fastest.
Arguments:
- query: bfloat16 [2, 16384, 4096], P(None, 'ctx', 'head'), may hold values from -12 to 12
- key_in: bfloat16 [2, 16384, 4096], P(None, 'ctx', 'head'), may hold values from -12 to 12
- value: bfloat16 [2, 16384, 4096], P(None, 'ctx', 'head'), may hold values from -6 to 6
- rates: float32 [2, 8, 16384], P(None, 'head', 'ctx'), may hold values from 0.03 to 0.3
- w_in: bfloat16 [8, 512, 512], P('head'), may hold values from -50 to 50
- w_gate: bfloat16 [8, 512, 512], P('head'), may hold values from -50 to 50
- w_out: bfloat16 [8, 512, 512], P('head'), may hold values from -50 to 50
- norm_gain: float32 [8, 512], P('head'), may hold values from 0.1 to 1.9
- proj_weight: bfloat16 [4096, 5120], P('head'), may hold values from -0.125 to 0.125
Outputs:
- mixed: bfloat16 [2, 16384, 5120], P(None, 'ctx', 'head')
- new_in: bfloat16 [8, 512, 512], P('head')
- new_gate: bfloat16 [8, 512, 512], P('head')
- new_out: bfloat16 [8, 512, 512], P('head')
All inputs are finite; a program needn't handle non-finite values.
Results may differ from a plain program's by a relative error of at most 0.015.
Values may be sent and summed in bfloat16 or wider, within the bound.
A program may use at most 128 MiB of HBM per device.

v0:
```python
import jax
import jax.numpy as jnp
from jax import lax
from jax.sharding import PartitionSpec as P

DH = 512
HID = 512
GROUPS = 2
WINDOW = 1024


def with_halo(value, sides, width):
    for axis, dim in sides:
        peers, length = (lax.axis_size(axis), value.shape[dim])
        up = [(i, (i + 1) % peers) for i in range(peers - 1)]
        down = [(j, i) for i, j in up]
        last = lax.slice_in_dim(value, length - width, length, axis=dim)
        initial = lax.slice_in_dim(value, 0, width, axis=dim)
        before = lax.ppermute(last, axis, up)
        after = lax.ppermute(initial, axis, down)
        value = jnp.concatenate([before, value, after], axis=dim)
    return value


def silu_pair(inputs):
    sigmoid = jax.nn.sigmoid(inputs)
    return (inputs * sigmoid, sigmoid * (1.0 + inputs * (1.0 - sigmoid)))


def local_window(query_rows, extended, first_row, total_rows):
    tok_rows = query_rows.shape[0]
    half_window = WINDOW // 2
    block = min(512, tok_rows)
    key_rows = extended[0]
    value_rows = extended[1]
    row_ids = jnp.arange(block, dtype=jnp.int32)[:, None]
    col_ids = jnp.arange(block + WINDOW, dtype=jnp.int32)[None, :]

    def one_block(block_idx):
        offset = block_idx * block
        scores = jnp.dot(query_rows, key_rows.T, preferred_element_type=jnp.float32) * DH ** (-0.5)
        key_glob = first_row + offset + col_ids - half_window
        valid = (
            (col_ids - row_ids >= 0)
            & (col_ids - row_ids < WINDOW)
            & (key_glob >= 0)
            & (key_glob < total_rows)
        )
        scores = jnp.where(valid, scores, -1e30)
        largest = jnp.max(scores, axis=1, keepdims=True)
        expo = jnp.exp(scores - largest)
        probs = expo / jnp.sum(expo, axis=1, keepdims=True)
        return jnp.dot(probs.astype(jnp.bfloat16), value_rows, preferred_element_type=jnp.float32)

    outputs = lax.map(one_block, jnp.arange(tok_rows // block, dtype=jnp.int32))
    return outputs.reshape(tok_rows, query_rows.shape[1])


def column_scale(before, square_sums):
    kept = jnp.sqrt(jnp.sum(before * before, axis=0, keepdims=True))
    return kept / jnp.sqrt(square_sums[None, :] + 1e-06)


def local(query, key_in, value, rates, w_in, w_gate, w_out, norm_gain, proj_weight):
    tok_rows = query.shape[1]
    ctx_count = lax.axis_size("ctx")
    total_rows = tok_rows * ctx_count
    first_row = lax.axis_index("ctx") * tok_rows
    half_window = WINDOW // 2
    scale_in = DH ** (-0.5)
    scale_out = HID ** (-0.5)
    state = (
        w_in[0].astype(jnp.float32),
        w_gate[0].astype(jnp.float32),
        w_out[0].astype(jnp.float32),
    )
    gain_row = norm_gain[0]
    stacked = jnp.stack((key_in, value), axis=0)
    mixed_list = []
    for group_idx in range(GROUPS):
        query_rows = query[group_idx]
        key_rows = key_in[group_idx]
        value_rows = value[group_idx]
        rate_row = rates[group_idx, 0]
        extended = with_halo(stacked[:, group_idx], (("ctx", 1),), half_window)
        window = local_window(query_rows, extended, first_row, total_rows)
        bf_in = state[0].astype(jnp.bfloat16)
        bf_gate = state[1].astype(jnp.bfloat16)
        bf_out = state[2].astype(jnp.bfloat16)
        first_pre = jnp.dot(query_rows, bf_in, preferred_element_type=jnp.float32) * scale_in
        gate_pre = jnp.dot(query_rows, bf_gate, preferred_element_type=jnp.float32) * scale_in
        first_act, unused = silu_pair(first_pre)
        hidden_q = (first_act * gate_pre).astype(jnp.bfloat16)
        ttt_out = jnp.dot(hidden_q, bf_out, preferred_element_type=jnp.float32) * scale_out
        normed = (
            ttt_out
            * lax.rsqrt(jnp.mean(ttt_out * ttt_out, axis=1, keepdims=True) + 1e-06)
            * gain_row[None, :]
        )
        head_out = (normed + window).astype(jnp.bfloat16)
        key_first = jnp.dot(key_rows, bf_in, preferred_element_type=jnp.float32) * scale_in
        key_gate = jnp.dot(key_rows, bf_gate, preferred_element_type=jnp.float32) * scale_in
        key_act, key_slope = silu_pair(key_first)
        hidden_k = (key_act * key_gate).astype(jnp.bfloat16)
        scaled = (rate_row[:, None] * value_rows.astype(jnp.float32)).astype(jnp.bfloat16)
        grad_out = -scale_out * jnp.dot(hidden_k.T, scaled, preferred_element_type=jnp.float32)
        back = -scale_out * jnp.dot(scaled, bf_out.T, preferred_element_type=jnp.float32)
        delta_in = (back * key_gate * key_slope).astype(jnp.bfloat16)
        delta_gate = (back * key_act).astype(jnp.bfloat16)
        grad_in = scale_in * jnp.dot(key_rows.T, delta_in, preferred_element_type=jnp.float32)
        grad_gate = scale_in * jnp.dot(key_rows.T, delta_gate, preferred_element_type=jnp.float32)
        terms = jnp.dot(head_out, proj_weight, preferred_element_type=jnp.float32)
        mixed_rows = lax.psum_scatter(
            terms.astype(jnp.bfloat16), "head", scatter_dimension=1, tiled=True
        )
        mixed_list.append(mixed_rows)
        grads = lax.psum((grad_in, grad_gate, grad_out), "ctx")
        next_state = []
        for before, summed in zip(state, grads):
            changed = before - summed
            next_state.append(changed * column_scale(before, jnp.sum(changed * changed, axis=0)))
        state = tuple(next_state)
    mixed = jnp.stack(mixed_list, axis=0)
    return (
        mixed,
        state[0][None].astype(jnp.bfloat16),
        state[1][None].astype(jnp.bfloat16),
        state[2][None].astype(jnp.bfloat16),
    )


def solution(mesh):
    return jax.shard_map(
        local,
        mesh=mesh,
        in_specs=(
            P(None, "ctx", "head"),
            P(None, "ctx", "head"),
            P(None, "ctx", "head"),
            P(None, "head", "ctx"),
            P("head", None, None),
            P("head", None, None),
            P("head", None, None),
            P("head", None),
            P("head", None),
        ),
        out_specs=(
            P(None, "ctx", "head"),
            P("head", None, None),
            P("head", None, None),
            P("head", None, None),
        ),
        check_vma=False,
    )
```

profile of v0, /device:TPU:1, one launch (start us, length us, event | category | flops | bytes accessed | tf_op | source)
XLA Modules:
  0.0 783.9 jit_solution(1341425014134983942)
XLA Ops:
  8.9 1.7 convolution_multiply_fusion.13
  10.6 1.7 convolution_multiply_fusion.14
  12.9 1.7 convolution_multiply_fusion.8
  14.6 1.7 fusion.21
  19.3 6.2 collective-permute-start
  25.4 1.9 collective-permute-start.1
  28.4 2.0 copy.35
  33.9 272.7 %all-reduce.7.cloned.1.call-done = (f32[512,512]{0,1:T(8,128)}, f32[512,512]{0,1:T(8,128)}, f32[512,512]{0,1:T(8,128)}) async-done(((f32[512,512]{0,1:T(8,128)}, f32[512,512]{0,1:T(8,128)}, f32[512,512]{0,1:T(8,128)}), (f32[512,512]{0,1:T(8,128)}, f32[512,512]{0,1:T(8,128)}, f32[512,512]{0,1:T(8,128)})) %all-reduce.7.cloned.1.call-update) | async-done | bytes 3145744 | tf_op jit(solution)/shard_map/psum | solution.py:117
  306.6 2.5 multiply_reduce_fusion.7
  310.9 1.7 convolution_multiply_fusion.2
  313.2 1.6 fusion.14
  316.5 3.8 fusion.30
  320.4 2.6 copy.36
  324.4 2.0 pad_maximum_fusion
  328.1 1.7 copy-done.9
  330.3 10.5 %convolution_convert_fusion.1 = bf16[512,5120]{1,0:T(8,128)(2,1)} fusion(bf16[512,5120]{1,0:T(8,128)(2,1)} %param.17, bf16[2,1536,512]{2,1,0:T(8,128)(2,1)} %copy-done.8, f32[512,1536]{0,1:T(8,128)} %copy-done.9, f32[512]{0:T(512)S(1)} %fusion.9, f32[512]{0:T(512)S(1)} %get-tuple-element.87, f32[512,512]{0,1:T(8,128)} %fusion.30, f32[512]{0:T(512)S(1)} %bitcast.177, ...), kind=kOutput, calls=%fused_computation.1 | convolution fusion | flops 3495690240 | bytes 16261120 | tf_op jit(solution)/shard_map/dot_general | solution.py:112
  340.9 8.0 %copy.55 = bf16[512,5120]{0,1:T(8,128)(2,1)} copy(bf16[512,5120]{1,0:T(8,128)(2,1)} %convolution_convert_fusion.1) | data formatting | bytes 10485760
  348.9 2.1 collective-permute-start.2
  351.0 2.7 collective-permute-start.3
  353.7 41.9 %collective-permute-done.2 = bf16[2,512,512]{2,1,0:T(8,128)(2,1)S(1)} collective-permute-done((bf16[2,512,512]{2,1,0:T(8,128)(2,1)}, bf16[2,512,512]{2,1,0:T(8,128)(2,1)S(1)}, u32[]{:S(2)}, u32[]{:S(2)}) %collective-permute-start.2) | collective-permute-done | bytes 1048608 | tf_op jit(solution)/shard_map/ppermute | solution.py:19
  398.5 1.7 copy-done.7
  402.1 3.4 fusion.29
  405.5 2.5 copy.43
  409.5 10.6 %convolution_convert_fusion = bf16[512,5120]{1,0:T(8,128)(2,1)} fusion(bf16[512,5120]{1,0:T(8,128)(2,1)} %param.17, bf16[2,1536,512]{2,1,0:T(8,128)(2,1)} %copy-done.6, f32[512,1536]{0,1:T(8,128)} %copy-done.7, f32[512]{0:T(512)S(1)} %fusion.10, f32[512]{0:T(512)S(1)} %get-tuple-element.85, f32[512,512]{0,1:T(8,128)} %fusion.29, ...), kind=kOutput, calls=%fused_computation | convolution fusion | flops 3495690240 | bytes 16261120 | tf_op jit(solution)/shard_map/dot_general | solution.py:112
  420.1 7.9 %copy.57 = bf16[512,5120]{0,1:T(8,128)(2,1)} copy(bf16[512,5120]{1,0:T(8,128)(2,1)} %convolution_convert_fusion) | data formatting | bytes 10485760
  428.0 330.9 %all-reduce.5.cloned.1.call-done = (f32[512,512]{0,1:T(8,128)}, f32[512,512]{0,1:T(8,128)}, f32[512,512]{0,1:T(8,128)}) async-done(((f32[512,512]{0,1:T(8,128)}, f32[512,512]{0,1:T(8,128)}, f32[512,512]{0,1:T(8,128)}), (f32[512,512]{0,1:T(8,128)}, f32[512,512]{0,1:T(8,128)}, f32[512,512]{0,1:T(8,128)})) %all-reduce.5.cloned.1.call-update) | async-done | bytes 3145744 | tf_op jit(solution)/shard_map/psum | solution.py:117
  759.0 1.6 multiply_reduce_fusion.1
  760.6 2.2 fusion.55
  762.8 2.0 copy.48
  764.9 1.7 multiply_reduce_fusion.3
  766.5 2.2 fusion.54
  768.8 2.0 copy.47
  (87 shorter events, 28.5 us)
Async XLA Ops:
  8.0 4.3 copy-start.10
  8.0 4.3 copy-start.15
  8.0 298.6 %all-reduce.7.cloned.1.call-start = ((), (), s32[]{:S(2)}) async-start(), calls=%async_computation.5 | async-start | bytes 6291456 | tf_op jit(solution)/shard_map/psum | solution.py:117
  12.8 1.7 copy-start.1
  17.7 9.7 %copy-start.3 = (bf16[1,512,512]{2,1,0:T(8,128)(2,1)S(1)}, bf16[1,512,512]{2,1,0:T(8,128)(2,1)}, u32[]{:S(2)}) copy-start(bf16[1,512,512]{2,1,0:T(8,128)(2,1)} %param.14) | copy-start | bytes 1572868
  17.7 741.3 %all-reduce.5.cloned.1.call-start = ((), (), s32[]{:S(2)}) async-start(), calls=%async_computation.4 | async-start | bytes 6291456 | tf_op jit(solution)/shard_map/psum | solution.py:117
  17.7 12.7 %copy-start.4 = (bf16[1,512,512]{2,1,0:T(8,128)(2,1)S(1)}, bf16[1,512,512]{2,1,0:T(8,128)(2,1)}, u32[]{:S(2)}) copy-start(bf16[1,512,512]{2,1,0:T(8,128)(2,1)} %param.13) | copy-start | bytes 1572868
  19.3 12.2 %copy-start.12 = (bf16[2,512,512]{2,1,0:T(8,128)(2,1)S(1)}, bf16[2,512,512]{2,1,0:T(8,128)(2,1)}, u32[]{:S(2)}) copy-start(bf16[2,512,512]{2,1,0:T(8,128)(2,1)} %param.9) | copy-start | bytes 3145732
  19.3 305.1 %collective-permute-start = (bf16[2,512,512]{2,1,0:T(8,128)(2,1)}, bf16[2,512,512]{2,1,0:T(8,128)(2,1)}, u32[]{:S(2)}, u32[]{:S(2)}) collective-permute-start(bf16[2,512,512]{2,1,0:T(8,128)(2,1)} %get-tuple-element.78), channel_id=1, source_target_pairs={{0,8},{8,16},{16,24},{24,32},{32,40},{40,48},{48,56},{56,64},{64,7... | collective-permute-start | bytes 3145736 | tf_op jit(solution)/shard_map/ppermute | solution.py:19
  25.4 298.9 %collective-permute-start.1 = (bf16[2,512,512]{2,1,0:T(8,128)(2,1)}, bf16[2,512,512]{2,1,0:T(8,128)(2,1)}, u32[]{:S(2)}, u32[]{:S(2)}) collective-permute-start(bf16[2,512,512]{2,1,0:T(8,128)(2,1)} %get-tuple-element.78), channel_id=1, source_target_pairs={{8,0},{16,8},{24,16},{32,24},{40,32},{48,40},{56,48},{64,56},{72,6... | collective-permute-start | bytes 3145736 | tf_op jit(solution)/shard_map/ppermute | solution.py:20
  31.9 2.0 copy-start
  306.6 2.5 copy-start.2
  306.6 3.1 copy-start.16
  306.6 3.1 copy-start.17
  309.7 1.2 copy-start.11
  316.3 456.2 %reduce-scatter.7.cloned.1.call-start = ((), (), s32[]{:S(2)}) async-start(), calls=%async_computation.2 | async-start | bytes 5898240
  324.3 2.2 copy-start.13
  326.4 1.7 copy-start.8
  328.1 1.8 copy-start.9
  328.1 2.2 copy-start.18
  348.8 425.0 %reduce-scatter.9.cloned.1.call-start = ((), (), s32[]{:S(2)}) async-start(), calls=%async_computation.3 | async-start | bytes 5898240
  348.9 48.0 %copy-start.14 = (bf16[2,512,512]{2,1,0:T(8,128)(2,1)S(1)}, bf16[2,512,512]{2,1,0:T(8,128)(2,1)}, u32[]{:S(2)}) copy-start(bf16[2,512,512]{2,1,0:T(8,128)(2,1)} %param.9) | copy-start | bytes 3145732
  348.9 46.6 %collective-permute-start.2 = (bf16[2,512,512]{2,1,0:T(8,128)(2,1)}, bf16[2,512,512]{2,1,0:T(8,128)(2,1)S(1)}, u32[]{:S(2)}, u32[]{:S(2)}) collective-permute-start(bf16[2,512,512]{2,1,0:T(8,128)(2,1)} %get-tuple-element.79), channel_id=1, source_target_pairs={{0,8},{8,16},{16,24},{24,32},{32,40},{40,48},{48,56},{56,64},{64,7... | collective-permute-start | bytes 3145736 | tf_op jit(solution)/shard_map/ppermute | solution.py:19
  351.0 44.6 %collective-permute-start.3 = (bf16[2,512,512]{2,1,0:T(8,128)(2,1)}, bf16[2,512,512]{2,1,0:T(8,128)(2,1)S(1)}, u32[]{:S(2)}, u32[]{:S(2)}) collective-permute-start(bf16[2,512,512]{2,1,0:T(8,128)(2,1)} %get-tuple-element.79), channel_id=1, source_target_pairs={{8,0},{16,8},{24,16},{32,24},{40,32},{48,40},{56,48},{64,56},{72,6... | collective-permute-start | bytes 3145736 | tf_op jit(solution)/shard_map/ppermute | solution.py:20
  396.9 1.7 copy-start.6
  398.5 1.7 copy-start.7
  764.9 6.0 copy-start.5
Sparse Core Ops, SparseCore 0:
  17.8 288.7 all-reduce.6
  316.4 442.4 all-reduce.4
Sparse Core Ops, SparseCore 1:
  348.9 137.0 reduce-scatter.6
  488.5 121.8 reduce-scatter.8
where the time goes:
time: 785 us; the launch traced here: 784 us
  waiting for transfers between devices  646 us (82%)
  matrix products  47.6 us (6%)
  local copies, waits for them, and re-layouts  40.2 us (5%)
  other arithmetic  21.4 us (3%)
  between operations  15.8 us (2%)
  starting transfers between devices  13.2 us (2%)
    psum x2, waiting for transfers between devices, local(): grads = lax.psum((grad_in, grad_gate, grad_out), 'ctx')  604 us
    ppermute x2, waiting for transfers between devices, with_halo(): before = lax.ppermute(last, axis, up)  41.9 us
    unnamed x48, local copies, waits for them, and re-layouts  32.6 us
    dot_general x2, matrix products, local(): terms = jnp.dot(head_out, proj_weight, preferred_element_type=jnp.float32)  21.1 us
  transfers between devices with their start and end apart: 8, of which 3 were waited for; matrix products, arithmetic and copies ran while one was open for 12% of the time, Pallas kernels for 0%

commit v1 on v0

v1 whole, which is shorter than its diff:
```python
import functools

import jax
import jax.numpy as jnp
from jax import lax
from jax.experimental import pallas as pl
from jax.experimental.pallas import tpu as pltpu
from jax.sharding import PartitionSpec as P

DH = 512
HID = 512
HALF = HID // 2
GROUPS = 2
WINDOW = 1024
SIDE = WINDOW // 2
A = DH**-0.5
B = HID**-0.5
BF = jnp.bfloat16
F32 = jnp.float32


def dot(x, y, dims=((1,), (0,))):
    return lax.dot_general(x, y, (dims, ((), ())), preferred_element_type=F32)


def kernel(
    chips,
    ys,
    q_hbm,
    k_hbm,
    v_hbm,
    rates_ref,
    w1_ref,
    w3_ref,
    w2_ref,
    gain_ref,
    proj_hbm,
    mixed_ref,
    out1_ref,
    out3_ref,
    out2_ref,
    qs,
    kx,
    vx,
    rx,
    s13,
    s2,
    b13,
    b2,
    acc13,
    acc2,
    win,
    part,
    landed,
    total,
    gathered,
    heads,
    pw,
    xs,
    xr,
    xa,
    loc_sem,
    sib_s,
    sib_r,
    far_s,
    far_r,
    rs_s,
    rs_r,
    ag_s,
    ag_r,
    ex_s,
    ex_r,
    w_s,
    w_r,
    ws_s,
    ws_r,
    y_s,
    y_r,
    x_s,
    x_r,
):
    tok = kx.shape[1] - 2 * SIDE
    ctx = lax.axis_index("ctx")
    head = lax.axis_index("head")
    n_ctx = 2 * chips
    core = lax.rem(ctx, 2)
    chip = lax.div(ctx, 2)
    y = lax.div(head, 2)
    x_lo = lax.rem(head, 2)
    sib = (ctx + 1 - 2 * core, head)
    far = (lax.rem(ctx + 2 * core - 1 + n_ctx, n_ctx), head)
    pair = (ctx, head + 1 - 2 * x_lo)

    def chip_peer(d):
        return (lax.rem(chip + d, chips) * 2 + core, head)

    def y_peer(d):
        return (ctx, lax.rem(y + d, ys) * 2 + x_lo)

    peers = [sib, far, pair] + [chip_peer(d) for d in range(1, chips)] + [y_peer(d) for d in range(1, ys)]

    def local_copy(src, dst, n):
        c = pltpu.make_async_copy(src, dst, loc_sem.at[n])
        c.start()
        return c

    waiting = []

    def remote(src, dst, send, recv, peer):
        c = pltpu.make_async_remote_copy(
            src_ref=src, dst_ref=dst, send_sem=send, recv_sem=recv, device_id=peer, device_id_type=pl.DeviceIdType.MESH
        )
        c.start()
        waiting.append(c)
        return c

    own = pl.ds(SIDE, tok)
    my_half = pl.ds(pl.multiple_of(core * HALF, HALF), HALF)

    loads_k = [local_copy(k_hbm.at[g], kx.at[g, own], g) for g in range(GROUPS)]
    loads_v = [local_copy(v_hbm.at[g], vx.at[g, own], GROUPS + g) for g in range(GROUPS)]
    load_q = local_copy(q_hbm, qs, 2 * GROUPS)
    load_p = local_copy(proj_hbm.at[:, pl.ds(pl.multiple_of(y * 1280, 1280), 1280)], pw.at[0], 2 * GROUPS + 1)

    barrier = pltpu.get_barrier_semaphore()
    for peer in peers:
        pl.semaphore_signal(barrier, inc=1, device_id=peer, device_id_type=pl.DeviceIdType.MESH)
    pl.semaphore_wait(barrier, len(peers))

    to_sib = pl.ds(pl.multiple_of(core * WINDOW, SIDE), SIDE)
    to_far = pl.ds(pl.multiple_of((1 - core) * WINDOW, SIDE), SIDE)
    from_sib = pl.ds(pl.multiple_of((1 - core) * WINDOW, SIDE), SIDE)

    rate_copy = remote(rates_ref, rx, sib_s.at[2 * GROUPS], sib_r.at[2 * GROUPS], sib)
    sib_copies, far_copies = [], []
    for g in range(GROUPS):
        sib_copies.append(
            (
                remote(k_hbm.at[g], kx.at[g, to_sib], sib_s.at[2 * g], sib_r.at[2 * g], sib),
                remote(v_hbm.at[g], vx.at[g, to_sib], sib_s.at[2 * g + 1], sib_r.at[2 * g + 1], sib),
            )
        )
        far_copies.append(
            (
                remote(k_hbm.at[g], kx.at[g, to_far], far_s.at[2 * g], far_r.at[2 * g], far),
                remote(v_hbm.at[g], vx.at[g, to_far], far_s.at[2 * g + 1], far_r.at[2 * g + 1], far),
            )
        )
    w_copies = []
    for d in range(1, ys):
        cols = pl.ds(pl.multiple_of(lax.rem(y + d, ys) * 1280, 1280), 1280)
        w_copies.append(remote(proj_hbm.at[my_half, cols], pw.at[d, my_half], w_s.at[d], w_r.at[d], y_peer(d)))

    for c in range(2):
        cols = slice(c * HALF, (c + 1) * HALF)
        for j, w in enumerate((w1_ref, w3_ref)):
            into = slice(j * HALF, (j + 1) * HALF)
            b13[c, :, into] = w[:, cols]
            s13[c, :, into] = w[:, cols].astype(F32)
    b2[...] = w2_ref[...]
    s2[...] = w2_ref[...].astype(F32)

    def key_part(g, rows, rate_row, first):
        k = kx[g, rows]
        v = vx[g, rows]
        f = dot(k, b13[core]) * A
        f1, f3 = f[:, :HALF], f[:, HALF:]
        sig = jax.nn.sigmoid(f1)
        act = f1 * sig
        slope = sig * (1.0 + f1 * (1.0 - sig))
        hk = (act * f3).astype(BF)
        rate = jnp.transpose(jnp.broadcast_to(rate_row, (128, tok)))[:, :1]
        scaled = (v.astype(F32) * rate).astype(BF)
        back = dot(scaled, b2[my_half], ((1,), (1,))) * -B
        d13 = jnp.concatenate([(back * f3 * slope).astype(BF), (back * act).astype(BF)], axis=1)
        g2 = dot(hk, scaled, ((0,), (0,))) * -B
        g13 = dot(k, d13, ((0,), (0,))) * A
        if first:
            acc13[...] = g13
            acc2[...] = g2
        else:
            rows13, rows2 = DH // chips, HALF // chips
            part[g, :, :rows13] = (acc13[...] + g13).reshape(chips, rows13, 2 * HALF).astype(BF)
            part[g, :, rows13:] = (acc2[...] + g2).reshape(chips, rows2, DH).astype(BF)

    def gradients(g):
        if g == 0:
            loads_k[0].wait()
            loads_v[0].wait()
        key_part(g, own, rates_ref[g : g + 1], True)
        if g == 0:
            rate_copy.wait_recv()
            for c in sib_copies[0]:
                c.wait_recv()
        key_part(g, from_sib, rx[g : g + 1], False)
        return [
            remote(part.at[g, lax.rem(chip + d, chips)], landed.at[g, d], rs_s.at[g, d], rs_r.at[g, d], chip_peer(d))
            for d in range(1, chips)
        ]

    def reduce_own(g, copies):
        for c in copies:
            c.wait_recv()
        s = part[g, chip].astype(F32)
        for d in range(1, chips):
            s += landed[g, d].astype(F32)
        total[g] = s.astype(BF)
        gathered[g, core, chip] = total[g]
        return [
            remote(total.at[g], gathered.at[g, core, chip], ag_s.at[g, d], ag_r.at[g, d], chip_peer(d))
            for d in range(1, chips)
        ]

    def exchange(g, copies):
        for c in copies:
            c.wait_recv()
        return remote(gathered.at[g, core], gathered.at[g, core], ex_s.at[g], ex_r.at[g], sib)

    def rescaled(before, grad):
        changed = before - grad
        kept = jnp.sqrt(jnp.sum(before * before, axis=0, keepdims=True))
        return changed * (kept / jnp.sqrt(jnp.sum(changed * changed, axis=0, keepdims=True) + 1e-6))

    def update(g, copy):
        copy.wait_recv()
        rows13 = DH // chips
        for c in range(2):
            grad = gathered[g, c, :, :rows13].astype(F32).reshape(DH, 2 * HALF)
            new = rescaled(s13[c], grad)
            s13[c] = new
            b13[c] = new.astype(BF)
        grad = gathered[g, :, :, rows13:].astype(F32).reshape(HID, DH)
        new = rescaled(s2[...], grad)
        s2[...] = new
        b2[...] = new.astype(BF)

    block = 256
    width = block + WINDOW

    def attend(g):
        if g > 0:
            loads_k[g].wait()
            loads_v[g].wait()
        for c in far_copies[g]:
            c.wait_recv()
        if g > 0:
            for c in sib_copies[g]:
                c.wait_recv()

        @pl.loop(0, tok // block)
        def _(i):
            start = pl.multiple_of(i * block, block)
            q = qs[g, pl.ds(start, block)]
            s = dot(q, kx[g, pl.ds(start, width)], ((1,), (1,))) * A
            row = lax.broadcasted_iota(jnp.int32, (block, width), 0)
            col = lax.broadcasted_iota(jnp.int32, (block, width), 1)
            at = ctx * tok + start - SIDE + col
            seen = (col - row >= 0) & (col - row < WINDOW) & (at >= 0) & (at < n_ctx * tok)
            s = jnp.where(seen, s, -1e30)
            e = jnp.exp(s - jnp.max(s, axis=1, keepdims=True))
            o = dot(e.astype(BF), vx[g, pl.ds(start, width)])
            win[g, pl.ds(start, block)] = o / jnp.sum(e, axis=1, keepdims=True)

    def hidden(g, c):
        f = dot(qs[g], b13[c]) * A
        f1 = f[:, :HALF]
        return (f1 * jax.nn.sigmoid(f1) * f[:, HALF:]).astype(BF)

    def head_out(g):
        h = jnp.concatenate([hidden(g, 0), hidden(g, 1)], axis=1)
        t = dot(h, b2[...]) * B
        normed = t * lax.rsqrt(jnp.mean(t * t, axis=1, keepdims=True) + 1e-6) * gain_ref[...]
        heads[g, 0] = (normed + win[g]).astype(BF)
        return [remote(heads.at[g, 0], heads.at[g, d], y_s.at[g, d], y_r.at[g, d], y_peer(d)) for d in range(1, ys)]

    def project(g, copies):
        for c in copies:
            c.wait_recv()
        wide = 640
        for mine in (False, True):
            def cols_of(which):
                return slice(which * wide, (which + 1) * wide)

            for which in range(2):
                @pl.when((x_lo == which) if mine else (x_lo != which))
                def _():
                    t = dot(heads[g, 0], pw[0, :, cols_of(which)])
                    for d in range(1, ys):
                        t += dot(heads[g, d], pw[d, :, cols_of(which)])
                    if mine:
                        xa[g] = t
                    else:
                        xs[g] = t.astype(BF)

            if not mine:
                sent = remote(xs.at[g], xr.at[g], x_s.at[g], x_r.at[g], pair)
        return sent

    reducing = gradients(0)
    load_q.wait()
    attend(0)
    y_copies0 = head_out(0)
    summed = reduce_own(0, reducing)
    attend(1)
    ex = exchange(0, summed)
    update(0, ex)
    reducing = gradients(1)
    y_copies1 = head_out(1)
    w_forward = []
    for d in range(1, ys):
        w_copies[d - 1].wait_recv()
        w_forward.append(remote(pw.at[d, my_half], pw.at[d, my_half], ws_s.at[d], ws_r.at[d], sib))
    summed = reduce_own(1, reducing)
    load_p.wait()
    for c in w_forward:
        c.wait_recv()
    sent0 = project(0, y_copies0)
    ex = exchange(1, summed)
    sent1 = project(1, y_copies1)
    update(1, ex)
    for c in range(2):
        cols = slice(c * HALF, (c + 1) * HALF)
        out1_ref[:, cols] = b13[c, :, :HALF]
        out3_ref[:, cols] = b13[c, :, HALF:]
    out2_ref[...] = b2[...]
    for g, sent in ((0, sent0), (1, sent1)):
        sent.wait_recv()
        mixed_ref[g] = (xa[g] + xr[g].astype(F32)).astype(BF)
    for c in waiting:
        c.wait_send()


def local(query, key_in, value, rates, w_in, w_gate, w_out, norm_gain, proj_weight):
    tok = query.shape[1]
    chips = lax.axis_size("ctx") // 2
    ys = lax.axis_size("head") // 2
    piece = DH // chips + HALF // chips
    vmem = pl.BlockSpec(memory_space=pltpu.VMEM)
    hbm = pl.BlockSpec(memory_space=pl.ANY)
    dma = pltpu.SemaphoreType.DMA
    ext = tok + WINDOW
    mixed, new1, new3, new2 = pl.pallas_call(
        functools.partial(kernel, chips, ys),
        out_shape=(
            jax.ShapeDtypeStruct((GROUPS, tok, 640), BF),
            jax.ShapeDtypeStruct((DH, HID), BF),
            jax.ShapeDtypeStruct((DH, HID), BF),
            jax.ShapeDtypeStruct((HID, DH), BF),
        ),
        in_specs=[hbm, hbm, hbm, vmem, vmem, vmem, vmem, vmem, hbm],
        out_specs=(vmem, vmem, vmem, vmem),
        scratch_shapes=[
            pltpu.VMEM((GROUPS, tok, DH), BF),
            pltpu.VMEM((GROUPS, ext, DH), BF),
            pltpu.VMEM((GROUPS, ext, DH), BF),
            pltpu.VMEM((GROUPS, tok), F32),
            pltpu.VMEM((2, DH, 2 * HALF), F32),
            pltpu.VMEM((HID, DH), F32),
            pltpu.VMEM((2, DH, 2 * HALF), BF),
            pltpu.VMEM((HID, DH), BF),
            pltpu.VMEM((DH, 2 * HALF), F32),
            pltpu.VMEM((HALF, DH), F32),
            pltpu.VMEM((GROUPS, tok, DH), F32),
            pltpu.VMEM((GROUPS, chips, piece, DH), BF),
            pltpu.VMEM((GROUPS, chips, piece, DH), BF),
            pltpu.VMEM((GROUPS, piece, DH), BF),
            pltpu.VMEM((GROUPS, 2, chips, piece, DH), BF),
            pltpu.VMEM((GROUPS, ys, tok, DH), BF),
            pltpu.VMEM((ys, DH, 1280), BF),
            pltpu.VMEM((GROUPS, tok, 640), BF),
            pltpu.VMEM((GROUPS, tok, 640), BF),
            pltpu.VMEM((GROUPS, tok, 640), F32),
            dma((2 * GROUPS + 2,)),
            dma((2 * GROUPS + 1,)),
            dma((2 * GROUPS + 1,)),
            dma((2 * GROUPS,)),
            dma((2 * GROUPS,)),
            dma((GROUPS, chips)),
            dma((GROUPS, chips)),
            dma((GROUPS, chips)),
            dma((GROUPS, chips)),
            dma((GROUPS,)),
            dma((GROUPS,)),
            dma((ys,)),
            dma((ys,)),
            dma((ys,)),
            dma((ys,)),
            dma((GROUPS, ys)),
            dma((GROUPS, ys)),
            dma((GROUPS,)),
            dma((GROUPS,)),
        ],
        compiler_params=pltpu.CompilerParams(
            collective_id=0, has_side_effects=True, vmem_limit_bytes=60 * 1024 * 1024
        ),
    )(
        query,
        key_in,
        value,
        rates[:, 0],
        w_in[0],
        w_gate[0],
        w_out[0],
        norm_gain,
        proj_weight,
    )
    return mixed, new1[None], new3[None], new2[None]


def solution(mesh):
    return jax.shard_map(
        local,
        mesh=mesh,
        in_specs=(
            P(None, "ctx", "head"),
            P(None, "ctx", "head"),
            P(None, "ctx", "head"),
            P(None, "head", "ctx"),
            P("head", None, None),
            P("head", None, None),
            P("head", None, None),
            P("head", None),
            P("head", None),
        ),
        out_specs=(
            P(None, "ctx", "head"),
            P("head", None, None),
            P("head", None, None),
            P("head", None, None),
        ),
        check_vma=False,
    )
```

time: 785 us -> 157 us (0.20)
  waiting for transfers between devices: 646 us -> 0 us
  Pallas kernels: 0 us -> 149 us
  matrix products: 47.6 us -> 0 us
  local copies, waits for them, and re-layouts: 40.2 us -> 6.24 us
  other arithmetic: 21.4 us -> 0 us
  between operations: 15.8 us -> 0.66 us
  starting transfers between devices: 13.2 us -> 0 us
    psum x2 -> x0, waiting for transfers between devices: 604 us -> none  [local(): grads = lax.psum((grad_in, grad_gate, grad_out), 'ctx')]
    pallas_call x0 -> x1, Pallas kernels: none -> 149 us  [local(): pl.pallas_call(functools.partial(kernel, chips, ys), out_shape=(jax.Shape...]
    dot_general x20 -> x0, matrix products: 47.6 us -> none  [the longest x2 21.1 us: local(): terms = jnp.dot(head_out, proj_weight, preferred_element_type=jnp.float32)]
    ppermute x4 -> x0, waiting for transfers between devices: 41.9 us -> none  [the longest x2 41.9 us: with_halo(): before = lax.ppermute(last, axis, up)]
    unnamed x48 -> x11, local copies, waits for them, and re-layouts: 32.6 us -> 6.24 us
    ppermute x4 -> x0, starting transfers between devices: 12.8 us -> none  [the longest x2 8.22 us: with_halo(): before = lax.ppermute(last, axis, up)]
    reduce_sum x9 -> x0, other arithmetic: 10.3 us -> none  [the longest x3 3.66 us: column_scale(): kept = jnp.sqrt(jnp.sum(before * before, axis=0, keepdims=True))]
  transfers between devices with their start and end apart: 8 -> 0, of which waited for: 3 -> 0; matrix products, arithmetic and copies ran while one was open for 12% -> 0% of each run, Pallas kernels for 0% -> 0%
where the time goes in v1:
time: 157 us; the launch traced here: 156 us
  Pallas kernels  149 us (95%)
  local copies, waits for them, and re-layouts  6.24 us (4%)
    pallas_call x1, Pallas kernels, local(): pl.pallas_call(functools.partial(kernel, chips, ys), out_shape=(jax.Shape...  149 us
    unnamed x11, local copies, waits for them, and re-layouts  6.24 us

profile of v1, /device:TPU:1, one launch (start us, length us, event | category | flops | bytes accessed | tf_op | source)
XLA Modules:
  0.0 156.4 jit_solution(4130033707445977546)
XLA Ops:
  0.6 1.3 copy.15
  1.9 149.5 %shard_map.120 = (bf16[2,512,640]{2,1,0:T(8,128)(2,1)}, bf16[512,512]{1,0:T(8,128)(2,1)}, bf16[512,512]{1,0:T(8,128)(2,1)}, bf16[512,512]{1,0:T(8,128)(2,1)}) custom-call(bf16[2,512,512]{2,1,0:T(8,128)(2,1)} %q_hbm.1, bf16[2,512,512]{2,1,0:T(8,128)(2,1)} %k_hbm.1, bf16[2,512,512]{2,1,0:T(8,128)(2,1)} %v_hbm.1, f32[2,512]{1,0:T(2,128)} %bitcast.15, ...), custom_call_target="tpu_custom_call" | custom-call | tf_op jit(solution)/shard_map/pallas_call | solution.py:342
  151.4 0.0 copy-start.2
  151.4 0.0 copy-start.1
  151.4 2.6 %copy.20 = bf16[2,512,640]{2,1,0:T(8,128)(2,1)} copy(bf16[2,512,640]{2,1,0:T(8,128)(2,1)} %get-tuple-element.16) | data formatting | bytes 2621440
  154.0 0.0 copy-done.2
  154.0 0.0 copy-start
  154.0 0.8 copy.21
  154.8 0.0 copy-done.1
  154.8 0.8 copy.22
  155.6 0.0 copy-done
  155.6 0.8 copy.23
Async XLA Ops:
  151.4 2.6 %copy-start.2 = (bf16[512,512]{1,0:T(8,128)(2,1)S(1)}, bf16[512,512]{1,0:T(8,128)(2,1)}, u32[]{:S(2)}) copy-start(bf16[512,512]{1,0:T(8,128)(2,1)} %get-tuple-element.9) | copy-start | bytes 1572868
  151.4 3.4 %copy-start.1 = (bf16[512,512]{1,0:T(8,128)(2,1)S(1)}, bf16[512,512]{1,0:T(8,128)(2,1)}, u32[]{:S(2)}) copy-start(bf16[512,512]{1,0:T(8,128)(2,1)} %get-tuple-element.10) | copy-start | bytes 1572868
  154.0 1.6 %copy-start = (bf16[512,512]{1,0:T(8,128)(2,1)S(1)}, bf16[512,512]{1,0:T(8,128)(2,1)}, u32[]{:S(2)}) copy-start(bf16[512,512]{1,0:T(8,128)(2,1)} %get-tuple-element.11) | copy-start | bytes 1572868

commit v2 on v1

v2 whole, which is shorter than its diff:
```python
import functools

import jax
import jax.numpy as jnp
from jax import lax
from jax.experimental import pallas as pl
from jax.experimental.pallas import tpu as pltpu
from jax.sharding import PartitionSpec as P

DH = 512
HID = 512
HALF = HID // 2
GROUPS = 2
WINDOW = 1024
SIDE = WINDOW // 2
A = DH**-0.5
B = HID**-0.5
CHUNKS = 2
FAR_PARTS = 4
BF = jnp.bfloat16
F32 = jnp.float32


def dot(x, y, dims=((1,), (0,))):
    return lax.dot_general(x, y, (dims, ((), ())), preferred_element_type=F32)


def kernel(
    zs,
    ys,
    q_hbm,
    k_hbm,
    v_hbm,
    rates_ref,
    w1_ref,
    w3_ref,
    w2_ref,
    gain_ref,
    proj_hbm,
    mixed_ref,
    out1_ref,
    out3_ref,
    out2_ref,
    qs,
    kx,
    vx,
    rx,
    s13,
    s2,
    b13,
    b2,
    kept13,
    kept2,
    acc13,
    acc2,
    hq,
    normed,
    part,
    landed,
    mine,
    theirs,
    gathered,
    heads,
    pw,
    xs,
    xr,
    xa,
    loc_sem,
    sib_s,
    sib_r,
    far_s,
    far_r,
    rs_s,
    rs_r,
    hi_s,
    hi_r,
    ag_s,
    ag_r,
    ex_s,
    ex_r,
    w_s,
    w_r,
    ws_s,
    ws_r,
    y_s,
    y_r,
    x_s,
    x_r,
):
    tok = kx.shape[1] - 2 * SIDE
    wide = xs.shape[-1]
    block = tok // CHUNKS
    rows13, rows2 = DH // zs, HALF // zs
    piece = rows13 + rows2
    ctx = lax.axis_index("ctx")
    head = lax.axis_index("head")
    n_ctx = 4 * zs
    core = lax.rem(ctx, 2)
    x_hi = lax.rem(lax.div(ctx, 2), 2)
    z = lax.div(ctx, 4)
    y = lax.div(head, 2)
    x_lo = lax.rem(head, 2)
    sib = (ctx + 1 - 2 * core, head)
    far = (lax.rem(ctx + 2 * core - 1 + n_ctx, n_ctx), head)
    pair = (ctx, head + 1 - 2 * x_lo)
    across = (ctx + 2 - 4 * x_hi, head)

    def z_at(d):
        return lax.rem(z + d + zs, zs)

    along = [(z_at(d) * 4 + x_hi * 2 + core, head) for d in (1, -1)]

    def y_peer(d):
        return (ctx, lax.rem(y + d, ys) * 2 + x_lo)

    peers = [sib, far, pair, across] + along + [y_peer(d) for d in range(1, ys)]

    def local_copy(src, dst, n):
        c = pltpu.make_async_copy(src, dst, loc_sem.at[n])
        c.start()
        return c

    waiting = []

    def remote(src, dst, send, recv, peer):
        c = pltpu.make_async_remote_copy(
            src_ref=src, dst_ref=dst, send_sem=send, recv_sem=recv, device_id=peer, device_id_type=pl.DeviceIdType.MESH
        )
        c.start()
        waiting.append(c)
        return c

    own = pl.ds(SIDE, tok)
    my_half = pl.ds(pl.multiple_of(core * HALF, HALF), HALF)

    loads_k = [local_copy(k_hbm.at[g], kx.at[g, own], g) for g in range(GROUPS)]
    loads_v = [local_copy(v_hbm.at[g], vx.at[g, own], GROUPS + g) for g in range(GROUPS)]
    load_q = local_copy(q_hbm, qs, 2 * GROUPS)
    load_p = local_copy(
        proj_hbm.at[:, pl.ds(pl.multiple_of(y * 2 * wide, 2 * wide), 2 * wide)], pw.at[0], 2 * GROUPS + 1
    )

    barrier = pltpu.get_barrier_semaphore()
    for peer in peers:
        pl.semaphore_signal(barrier, inc=1, device_id=peer, device_id_type=pl.DeviceIdType.MESH)
    pl.semaphore_wait(barrier, len(peers))

    to_sib = pl.ds(pl.multiple_of(core * WINDOW, SIDE), SIDE)
    from_sib = pl.ds(pl.multiple_of((1 - core) * WINDOW, SIDE), SIDE)

    def send_rows(g):
        return [
            remote(k_hbm.at[g], kx.at[g, to_sib], sib_s.at[2 * g], sib_r.at[2 * g], sib),
            remote(v_hbm.at[g], vx.at[g, to_sib], sib_s.at[2 * g + 1], sib_r.at[2 * g + 1], sib),
        ]

    far_copies = [[], []]
    far_rows = tok // FAR_PARTS

    def send_far(g, parts):
        for n in parts:
            rows = pl.ds(pl.multiple_of((1 - core) * WINDOW + n * far_rows, far_rows), far_rows)
            for j, (src, dst) in enumerate(((k_hbm, kx), (v_hbm, vx))):
                far_copies[g].append(
                    remote(
                        src.at[g, n * far_rows : (n + 1) * far_rows],
                        dst.at[g, rows],
                        far_s.at[g, j, n],
                        far_r.at[g, j, n],
                        far,
                    )
                )

    rate_copy = remote(rates_ref, rx, sib_s.at[2 * GROUPS], sib_r.at[2 * GROUPS], sib)
    sib_copies = [send_rows(0)]
    send_far(0, (0, 1))
    sib_copies.append(send_rows(1))
    w_copies = []

    def send_weights(d):
        cols = pl.ds(pl.multiple_of(lax.rem(y + d, ys) * 2 * wide, 2 * wide), 2 * wide)
        w_copies.append(remote(proj_hbm.at[my_half, cols], pw.at[d, my_half], w_s.at[d], w_r.at[d], y_peer(d)))

    def column_norm(x):
        return jnp.sqrt(jnp.sum(x * x, axis=0, keepdims=True))

    for c in range(2):
        cols = slice(c * HALF, (c + 1) * HALF)
        for j, w in enumerate((w1_ref, w3_ref)):
            into = slice(j * HALF, (j + 1) * HALF)
            b13[c, :, into] = w[:, cols]
            s13[c, :, into] = w[:, cols].astype(F32)
    b2[...] = w2_ref[...]
    s2[...] = w2_ref[...].astype(F32)

    def norms():
        for c in range(2):
            kept13[c] = column_norm(s13[c])
        kept2[...] = column_norm(s2[...])

    def key_part(g, rows, rate_row, first):
        k = kx[g, rows]
        v = vx[g, rows]
        f = dot(k, b13[core]) * A
        f1, f3 = f[:, :HALF], f[:, HALF:]
        sig = jax.nn.sigmoid(f1)
        act = f1 * sig
        slope = sig * (1.0 + f1 * (1.0 - sig))
        hk = (act * f3).astype(BF)
        rate = jnp.transpose(jnp.broadcast_to(rate_row, (128, tok)))[:, :1]
        scaled = (v.astype(F32) * rate).astype(BF)
        back = dot(scaled, b2[my_half], ((1,), (1,))) * -B
        d13 = jnp.concatenate([(back * f3 * slope).astype(BF), (back * act).astype(BF)], axis=1)
        g2 = dot(hk, scaled, ((0,), (0,))) * -B
        g13 = dot(k, d13, ((0,), (0,))) * A
        if first:
            acc13[...] = g13
            acc2[...] = g2
        else:
            part[g, :, :rows13] = (acc13[...] + g13).reshape(zs, rows13, 2 * HALF).astype(BF)
            part[g, :, rows13:] = (acc2[...] + g2).reshape(zs, rows2, DH).astype(BF)

    def gradients(g):
        if g == 0:
            loads_k[0].wait()
            loads_v[0].wait()
        else:
            arrived(1)
        key_part(g, own, rates_ref[g : g + 1], True)
        if g == 0:
            rate_copy.wait_recv()
            for c in sib_copies[0]:
                c.wait_recv()
        key_part(g, from_sib, rx[g : g + 1], False)

    sub = piece // 2
    steps = zs // 2
    flows = ((0, 0), (1, 1), (0, 1), (1, 0))

    def rows_of(h):
        return pl.ds(h * sub, sub)

    def sum_gradients(g):
        last = {}
        for s in range(1, steps + 1):
            now = {}
            for way, h in flows:
                if s == 1 and way != h:
                    continue
                target = z_at((steps + 1 - s) * (1 - 2 * way))
                if (way, h) in last:
                    last[way, h].wait_recv()
                    got = landed[g, way, s - 2, h].astype(F32) + part[g, target, rows_of(h)].astype(F32)
                    landed[g, way, s - 2, h] = got.astype(BF)
                    src = landed.at[g, way, s - 2, h]
                else:
                    src = part.at[g, target, rows_of(h)]
                now[way, h] = remote(
                    src, landed.at[g, way, s - 1, h], rs_s.at[g, way, s - 1, h], rs_r.at[g, way, s - 1, h], along[way]
                )
            last = now
            yield
        swaps = []
        for h in range(2):
            for way in range(2):
                last[way, h].wait_recv()
            got = landed[g, 0, steps - 1, h].astype(F32) + landed[g, 1, steps - 1, h].astype(F32)
            mine[g, h] = (got + part[g, z, rows_of(h)].astype(F32)).astype(BF)
            swaps.append(remote(mine.at[g, h], theirs.at[g, h], hi_s.at[g, h], hi_r.at[g, h], across))
        yield
        exchanged = []

        def to_sibling(origin, h, n):
            at = gathered.at[g, core, origin, rows_of(h)]
            exchanged.append(remote(at, at, ex_s.at[g, n, h], ex_r.at[g, n, h], sib))

        last = {}
        for h in range(2):
            swaps[h].wait_recv()
            gathered[g, core, z, rows_of(h)] = (mine[g, h].astype(F32) + theirs[g, h].astype(F32)).astype(BF)
            for way in range(2):
                at = gathered.at[g, core, z, rows_of(h)]
                last[way, h] = remote(at, at, ag_s.at[g, way, 0, h], ag_r.at[g, way, 0, h], along[way])
            to_sibling(z, h, 0)
        yield
        for s in range(2, steps + 1):
            now = {}
            for way, h in flows:
                last[way, h].wait_recv()
                origin = z_at((s - 1) * (2 * way - 1))
                if s < steps or way == h:
                    at = gathered.at[g, core, origin, rows_of(h)]
                    now[way, h] = remote(
                        at, at, ag_s.at[g, way, s - 1, h], ag_r.at[g, way, s - 1, h], along[way]
                    )
                to_sibling(origin, h, 2 * (s - 1) - 1 + way)
            last = now
            yield
        for way in range(2):
            last[way, way].wait_recv()
            to_sibling(z_at(steps), way, zs - 1)
        for c in exchanged:
            c.wait_recv()

    def update(g):
        def rescaled(before, grad, kept):
            changed = before - grad
            return changed * (kept / jnp.sqrt(jnp.sum(changed * changed, axis=0, keepdims=True) + 1e-6))

        final = g == GROUPS - 1
        for c in range(2):
            grad = gathered[g, c, :, :rows13].astype(F32).reshape(DH, 2 * HALF)
            new = rescaled(s13[c], grad, kept13[c])
            if final:
                out1_ref[:, c * HALF : (c + 1) * HALF] = new[:, :HALF].astype(BF)
                out3_ref[:, c * HALF : (c + 1) * HALF] = new[:, HALF:].astype(BF)
            else:
                s13[c] = new
                b13[c] = new.astype(BF)
        grad = gathered[g, :, :, rows13:].astype(F32).reshape(HID, DH)
        new = rescaled(s2[...], grad, kept2[...])
        if final:
            out2_ref[...] = new.astype(BF)
        else:
            s2[...] = new
            b2[...] = new.astype(BF)

    done = set()

    def arrived(g):
        if g not in done:
            done.add(g)
            loads_k[g].wait()
            loads_v[g].wait()
            for c in sib_copies[g]:
                c.wait_recv()

    def hidden(g, c):
        f = dot(qs[g], b13[c]) * A
        f1 = f[:, :HALF]
        hq[:, c * HALF : (c + 1) * HALF] = (f1 * jax.nn.sigmoid(f1) * f[:, HALF:]).astype(BF)

    def fast_out():
        t = dot(hq[...], b2[...]) * B
        normed[...] = t * lax.rsqrt(jnp.mean(t * t, axis=1, keepdims=True) + 1e-6) * gain_ref[...]

    width = block + WINDOW
    y_copies = {}

    def attend(g, i):
        if i == 0:
            for c in far_copies[g]:
                c.wait_recv()
        start = i * block
        rows = slice(start, start + block)
        s = dot(qs[g, rows], kx[g, start : start + width], ((1,), (1,))) * A
        row = lax.broadcasted_iota(jnp.int32, (block, width), 0)
        col = lax.broadcasted_iota(jnp.int32, (block, width), 1)
        at = ctx * tok + start - SIDE + col
        seen = (col - row >= 0) & (col - row < WINDOW) & (at >= 0) & (at < n_ctx * tok)
        s = jnp.where(seen, s, -1e30)
        e = jnp.exp(s - jnp.max(s, axis=1, keepdims=True))
        o = dot(e.astype(BF), vx[g, start : start + width])
        window = o / jnp.sum(e, axis=1, keepdims=True)
        heads[g, 0, rows] = (normed[rows] + window).astype(BF)
        y_copies[g, i] = [
            remote(heads.at[g, 0, rows], heads.at[g, d, rows], y_s.at[g, i, d], y_r.at[g, i, d], y_peer(d))
            for d in range(1, ys)
        ]

    forwards = []

    def forward_weights():
        for d in range(1, ys):
            w_copies[d - 1].wait_recv()
            forwards.append(remote(pw.at[d, my_half], pw.at[d, my_half], ws_s.at[d], ws_r.at[d], sib))

    def weights_here():
        load_p.wait()
        for c in forwards:
            c.wait_recv()

    sent = {}

    def project(g, i, which):
        rows = slice(i * block, (i + 1) * block)
        cols = pl.ds(pl.multiple_of(which * wide, wide), wide)
        t = dot(heads[g, 0, rows], pw[0, :, cols])
        for d in range(1, ys):
            t += dot(heads[g, d, rows], pw[d, :, cols])
        return t

    def project_other(g, i):
        for c in y_copies[g, i]:
            c.wait_recv()
        xs[g, i] = project(g, i, 1 - x_lo).astype(BF)
        sent[g, i] = remote(xs.at[g, i], xr.at[g, i], x_s.at[g, i], x_r.at[g, i], pair)

    def project_own(g, i):
        xa[g, i] = project(g, i, x_lo)

    def finish(g, i):
        sent[g, i].wait_recv()
        mixed_ref[g, i * block : (i + 1) * block] = (xa[g, i] + xr[g, i].astype(F32)).astype(BF)

    def nothing():
        pass

    def interleave(steps_of, others):
        others = list(others)
        for _ in steps_of:
            if others:
                others.pop(0)()
        for other in others:
            other()

    norms()
    gradients(0)
    load_q.wait()
    interleave(
        sum_gradients(0),
        [
            lambda: (send_far(0, (2,)), send_weights(1), hidden(0, 0)),
            lambda: hidden(0, 1),
            lambda: (send_far(0, (3,)), send_weights(2), fast_out()),
            nothing,
            lambda: send_weights(3),
            lambda: send_far(1, (0,)),
            lambda: attend(0, 0),
            lambda: (send_far(1, (1,)), attend(0, 1)),
            nothing,
        ],
    )
    forward_weights()
    send_far(1, (2, 3))
    update(0)
    gradients(1)
    interleave(
        sum_gradients(1),
        [
            lambda: (weights_here(), project_other(0, 0), project_other(0, 1)),
            lambda: (hidden(1, 0), hidden(1, 1), fast_out()),
            lambda: attend(1, 0),
            lambda: attend(1, 1),
            lambda: (norms(), project_own(0, 0)),
            lambda: project_own(0, 1),
            lambda: project_other(1, 0),
            lambda: project_other(1, 1),
            lambda: (project_own(1, 0), project_own(1, 1)),
        ],
    )
    update(1)
    for g in range(GROUPS):
        for i in range(CHUNKS):
            finish(g, i)
    for c in waiting:
        c.wait_send()


def local(query, key_in, value, rates, w_in, w_gate, w_out, norm_gain, proj_weight):
    tok = query.shape[1]
    zs = lax.axis_size("ctx") // 4
    ys = lax.axis_size("head") // 2
    piece = DH // zs + HALF // zs
    wide = proj_weight.shape[1] // (2 * ys)
    vmem = pl.BlockSpec(memory_space=pltpu.VMEM)
    hbm = pl.BlockSpec(memory_space=pl.ANY)
    dma = pltpu.SemaphoreType.DMA
    ext = tok + WINDOW
    chunk = (GROUPS, CHUNKS, tok // CHUNKS, wide)
    mixed, new1, new3, new2 = pl.pallas_call(
        functools.partial(kernel, zs, ys),
        out_shape=(
            jax.ShapeDtypeStruct((GROUPS, tok, wide), BF),
            jax.ShapeDtypeStruct((DH, HID), BF),
            jax.ShapeDtypeStruct((DH, HID), BF),
            jax.ShapeDtypeStruct((HID, DH), BF),
        ),
        in_specs=[hbm, hbm, hbm, vmem, vmem, vmem, vmem, vmem, hbm],
        out_specs=(vmem, vmem, vmem, vmem),
        scratch_shapes=[
            pltpu.VMEM((GROUPS, tok, DH), BF),
            pltpu.VMEM((GROUPS, ext, DH), BF),
            pltpu.VMEM((GROUPS, ext, DH), BF),
            pltpu.VMEM((GROUPS, tok), F32),
            pltpu.VMEM((2, DH, 2 * HALF), F32),
            pltpu.VMEM((HID, DH), F32),
            pltpu.VMEM((2, DH, 2 * HALF), BF),
            pltpu.VMEM((HID, DH), BF),
            pltpu.VMEM((2, 1, 2 * HALF), F32),
            pltpu.VMEM((1, DH), F32),
            pltpu.VMEM((DH, 2 * HALF), F32),
            pltpu.VMEM((HALF, DH), F32),
            pltpu.VMEM((tok, HID), BF),
            pltpu.VMEM((tok, DH), F32),
            pltpu.VMEM((GROUPS, zs, piece, DH), BF),
            pltpu.VMEM((GROUPS, 2, zs // 2, 2, piece // 2, DH), BF),
            pltpu.VMEM((GROUPS, 2, piece // 2, DH), BF),
            pltpu.VMEM((GROUPS, 2, piece // 2, DH), BF),
            pltpu.VMEM((GROUPS, 2, zs, piece, DH), BF),
            pltpu.VMEM((GROUPS, ys, tok, DH), BF),
            pltpu.VMEM((ys, DH, 2 * wide), BF),
            pltpu.VMEM(chunk, BF),
            pltpu.VMEM(chunk, BF),
            pltpu.VMEM(chunk, F32),
            dma((2 * GROUPS + 2,)),
            dma((2 * GROUPS + 1,)),
            dma((2 * GROUPS + 1,)),
            dma((GROUPS, 2, FAR_PARTS)),
            dma((GROUPS, 2, FAR_PARTS)),
            dma((GROUPS, 2, zs // 2, 2)),
            dma((GROUPS, 2, zs // 2, 2)),
            dma((GROUPS, 2)),
            dma((GROUPS, 2)),
            dma((GROUPS, 2, zs // 2, 2)),
            dma((GROUPS, 2, zs // 2, 2)),
            dma((GROUPS, zs, 2)),
            dma((GROUPS, zs, 2)),
            dma((ys,)),
            dma((ys,)),
            dma((ys,)),
            dma((ys,)),
            dma((GROUPS, CHUNKS, ys)),
            dma((GROUPS, CHUNKS, ys)),
            dma((GROUPS, CHUNKS)),
            dma((GROUPS, CHUNKS)),
        ],
        compiler_params=pltpu.CompilerParams(
            collective_id=0, has_side_effects=True, vmem_limit_bytes=60 * 1024 * 1024
        ),
    )(
        query,
        key_in,
        value,
        rates[:, 0],
        w_in[0],
        w_gate[0],
        w_out[0],
        norm_gain,
        proj_weight,
    )
    return mixed, new1[None], new3[None], new2[None]


def solution(mesh):
    return jax.shard_map(
        local,
        mesh=mesh,
        in_specs=(
            P(None, "ctx", "head"),
            P(None, "ctx", "head"),
            P(None, "ctx", "head"),
            P(None, "head", "ctx"),
            P("head", None, None),
            P("head", None, None),
            P("head", None, None),
            P("head", None),
            P("head", None),
        ),
        out_specs=(
            P(None, "ctx", "head"),
            P("head", None, None),
            P("head", None, None),
            P("head", None, None),
        ),
        check_vma=False,
    )
```

time: 157 us -> 128 us (0.82)
  Pallas kernels: 149 us -> 120 us
    pallas_call x1, Pallas kernels: 149 us -> 120 us  [local(): pl.pallas_call(functools.partial(kernel, zs, ys), out_shape=(jax.ShapeDty...]
where the time goes in v2:
time: 128 us; the launch traced here: 126 us
  Pallas kernels  120 us (94%)
  local copies, waits for them, and re-layouts  6.24 us (5%)
    pallas_call x1, Pallas kernels, local(): pl.pallas_call(functools.partial(kernel, zs, ys), out_shape=(jax.ShapeDty...  120 us
    unnamed x11, local copies, waits for them, and re-layouts  6.24 us

profile of v2, /device:TPU:1, one launch (start us, length us, event | category | flops | bytes accessed | tf_op | source)
XLA Modules:
  0.0 126.5 jit_solution(11173471103030836295)
XLA Ops:
  0.6 1.3 %copy.15 = f32[2,1,512]{2,0,1:T(2,128)} copy(f32[2,1,512]{2,1,0:T(1,128)} %param.12) | data formatting | bytes 8192
  1.9 119.6 %shard_map.120 = (bf16[2,512,640]{2,1,0:T(8,128)(2,1)}, bf16[512,512]{1,0:T(8,128)(2,1)}, bf16[512,512]{1,0:T(8,128)(2,1)}, bf16[512,512]{1,0:T(8,128)(2,1)}) custom-call(bf16[2,512,512]{2,1,0:T(8,128)(2,1)} %q_hbm.1, bf16[2,512,512]{2,1,0:T(8,128)(2,1)} %k_hbm.1, bf16[2,512,512]{2,1,0:T(8,128)(2,1)} %v_hbm.1, f32[2,512]{1,0:T(2,128)} %bitcast.15, ...), custom_call_target="tpu_custom_call" | custom-call | tf_op jit(solution)/shard_map/pallas_call | solution.py:471
  121.5 0.0 copy-start.2
  121.5 0.0 copy-start.1
  121.5 2.6 %copy.20 = bf16[2,512,640]{2,1,0:T(8,128)(2,1)} copy(bf16[2,512,640]{2,1,0:T(8,128)(2,1)} %get-tuple-element.16) | data formatting | bytes 2621440
  124.1 0.0 copy-done.2
  124.1 0.0 copy-start
  124.1 0.8 copy.21
  124.9 0.0 copy-done.1
  124.9 0.8 copy.22
  125.7 0.0 copy-done
  125.7 0.8 copy.23
Async XLA Ops:
  121.5 2.6 %copy-start.2 = (bf16[512,512]{1,0:T(8,128)(2,1)S(1)}, bf16[512,512]{1,0:T(8,128)(2,1)}, u32[]{:S(2)}) copy-start(bf16[512,512]{1,0:T(8,128)(2,1)} %get-tuple-element.9) | copy-start | bytes 1572868
  121.5 3.4 %copy-start.1 = (bf16[512,512]{1,0:T(8,128)(2,1)S(1)}, bf16[512,512]{1,0:T(8,128)(2,1)}, u32[]{:S(2)}) copy-start(bf16[512,512]{1,0:T(8,128)(2,1)} %get-tuple-element.10) | copy-start | bytes 1572868
  124.1 1.6 %copy-start = (bf16[512,512]{1,0:T(8,128)(2,1)S(1)}, bf16[512,512]{1,0:T(8,128)(2,1)}, u32[]{:S(2)}) copy-start(bf16[512,512]{1,0:T(8,128)(2,1)} %get-tuple-element.11) | copy-start | bytes 1572868

commit v3 on v2

--- a/solution.py
+++ b/solution.py
@@ -143,6 +143,24 @@
     barrier = pltpu.get_barrier_semaphore()
     for peer in peers:
         pl.semaphore_signal(barrier, inc=1, device_id=peer, device_id_type=pl.DeviceIdType.MESH)
+    def column_norm(x):
+        return jnp.sqrt(jnp.sum(x * x, axis=0, keepdims=True))
+
+    for c in range(2):
+        cols = slice(c * HALF, (c + 1) * HALF)
+        for j, w in enumerate((w1_ref, w3_ref)):
+            into = slice(j * HALF, (j + 1) * HALF)
+            b13[c, :, into] = w[:, cols]
+            s13[c, :, into] = w[:, cols].astype(F32)
+    b2[...] = w2_ref[...]
+    s2[...] = w2_ref[...].astype(F32)
+
+    def norms():
+        for c in range(2):
+            kept13[c] = column_norm(s13[c])
+        kept2[...] = column_norm(s2[...])
+
+    norms()
     pl.semaphore_wait(barrier, len(peers))
 
     to_sib = pl.ds(pl.multiple_of(core * WINDOW, SIDE), SIDE)
@@ -180,23 +198,6 @@
     def send_weights(d):
         cols = pl.ds(pl.multiple_of(lax.rem(y + d, ys) * 2 * wide, 2 * wide), 2 * wide)
         w_copies.append(remote(proj_hbm.at[my_half, cols], pw.at[d, my_half], w_s.at[d], w_r.at[d], y_peer(d)))
-
-    def column_norm(x):
-        return jnp.sqrt(jnp.sum(x * x, axis=0, keepdims=True))
-
-    for c in range(2):
-        cols = slice(c * HALF, (c + 1) * HALF)
-        for j, w in enumerate((w1_ref, w3_ref)):
-            into = slice(j * HALF, (j + 1) * HALF)
-            b13[c, :, into] = w[:, cols]
-            s13[c, :, into] = w[:, cols].astype(F32)
-    b2[...] = w2_ref[...]
-    s2[...] = w2_ref[...].astype(F32)
-
-    def norms():
-        for c in range(2):
-            kept13[c] = column_norm(s13[c])
-        kept2[...] = column_norm(s2[...])
 
     def key_part(g, rows, rate_row, first):
         k = kx[g, rows]
@@ -302,28 +303,34 @@
         for c in exchanged:
             c.wait_recv()
 
-    def update(g):
-        def rescaled(before, grad, kept):
-            changed = before - grad
-            return changed * (kept / jnp.sqrt(jnp.sum(changed * changed, axis=0, keepdims=True) + 1e-6))
-
-        final = g == GROUPS - 1
+    def rescaled(before, grad, kept):
+        changed = before - grad
+        return changed * (kept / jnp.sqrt(jnp.sum(changed * changed, axis=0, keepdims=True) + 1e-6))
+
+    def new13(g, c):
+        grad = gathered[g, c, :, :rows13].astype(F32).reshape(DH, 2 * HALF)
+        return rescaled(s13[c], grad, kept13[c])
+
+    def new2(g):
+        grad = gathered[g, :, :, rows13:].astype(F32).reshape(HID, DH)
+        return rescaled(s2[...], grad, kept2[...])
+
+    def update13(c):
+        new = new13(0, c)
+        s13[c] = new
+        b13[c] = new.astype(BF)
+
+    def update2():
+        new = new2(0)
+        s2[...] = new
+        b2[...] = new.astype(BF)
+
+    def last_update():
         for c in range(2):
-            grad = gathered[g, c, :, :rows13].astype(F32).reshape(DH, 2 * HALF)
-            new = rescaled(s13[c], grad, kept13[c])
-            if final:
-                out1_ref[:, c * HALF : (c + 1) * HALF] = new[:, :HALF].astype(BF)
-                out3_ref[:, c * HALF : (c + 1) * HALF] = new[:, HALF:].astype(BF)
-            else:
-                s13[c] = new
-                b13[c] = new.astype(BF)
-        grad = gathered[g, :, :, rows13:].astype(F32).reshape(HID, DH)
-        new = rescaled(s2[...], grad, kept2[...])
-        if final:
-            out2_ref[...] = new.astype(BF)
-        else:
-            s2[...] = new
-            b2[...] = new.astype(BF)
+            new = new13(1, c)
+            out1_ref[:, c * HALF : (c + 1) * HALF] = new[:, :HALF].astype(BF)
+            out3_ref[:, c * HALF : (c + 1) * HALF] = new[:, HALF:].astype(BF)
+        out2_ref[...] = new2(1).astype(BF)
 
     done = set()
 
@@ -414,42 +421,42 @@
         for other in others:
             other()
 
-    norms()
+    for d in range(1, ys):
+        send_weights(d)
     gradients(0)
     load_q.wait()
     interleave(
         sum_gradients(0),
         [
-            lambda: (send_far(0, (2,)), send_weights(1), hidden(0, 0)),
-            lambda: hidden(0, 1),
-            lambda: (send_far(0, (3,)), send_weights(2), fast_out()),
+            lambda: (send_far(0, (2, 3)), hidden(0, 0)),
+            lambda: (hidden(0, 1), fast_out()),
             nothing,
-            lambda: send_weights(3),
-            lambda: send_far(1, (0,)),
+            nothing,
             lambda: attend(0, 0),
-            lambda: (send_far(1, (1,)), attend(0, 1)),
-            nothing,
+            lambda: (send_far(1, (0,)), attend(0, 1)),
+            lambda: send_far(1, (1,)),
+            lambda: (forward_weights(), send_far(1, (2, 3))),
+            lambda: (weights_here(), project_other(0, 0)),
         ],
     )
-    forward_weights()
-    send_far(1, (2, 3))
-    update(0)
+    update13(core)
+    update2()
     gradients(1)
     interleave(
         sum_gradients(1),
         [
-            lambda: (weights_here(), project_other(0, 0), project_other(0, 1)),
-            lambda: (hidden(1, 0), hidden(1, 1), fast_out()),
-            lambda: attend(1, 0),
+            lambda: (update13(1 - core), hidden(1, 0), hidden(1, 1), fast_out(), attend(1, 0)),
             lambda: attend(1, 1),
+            lambda: project_other(0, 1),
             lambda: (norms(), project_own(0, 0)),
             lambda: project_own(0, 1),
             lambda: project_other(1, 0),
             lambda: project_other(1, 1),
+            nothing,
             lambda: (project_own(1, 0), project_own(1, 1)),
         ],
     )
-    update(1)
+    last_update()
     for g in range(GROUPS):
         for i in range(CHUNKS):
             finish(g, i)

time: 128 us -> 112 us (0.88); the launches traced: 126 us -> 112 us
  Pallas kernels: 120 us -> 105 us
    pallas_call x1, Pallas kernels: 120 us -> 105 us  [local(): pl.pallas_call(functools.partial(kernel, zs, ys), out_shape=(jax.ShapeDty...]
where the time goes in v3:
time: 112 us
  Pallas kernels  105 us (94%)
  local copies, waits for them, and re-layouts  6.24 us (6%)
    pallas_call x1, Pallas kernels, local(): pl.pallas_call(functools.partial(kernel, zs, ys), out_shape=(jax.ShapeDty...  105 us
    unnamed x11, local copies, waits for them, and re-layouts  6.24 us

profile of v3, /device:TPU:1, one launch (start us, length us, event | category | flops | bytes accessed | tf_op | source)
XLA Modules:
  0.0 112.2 jit_solution(18117049810943698867)
XLA Ops:
  0.6 1.3 %copy.15 = f32[2,1,512]{2,0,1:T(2,128)} copy(f32[2,1,512]{2,1,0:T(1,128)} %param.12) | data formatting | bytes 8192
  1.9 105.3 %shard_map.120 = (bf16[2,512,640]{2,1,0:T(8,128)(2,1)}, bf16[512,512]{1,0:T(8,128)(2,1)}, bf16[512,512]{1,0:T(8,128)(2,1)}, bf16[512,512]{1,0:T(8,128)(2,1)}) custom-call(bf16[2,512,512]{2,1,0:T(8,128)(2,1)} %q_hbm.1, bf16[2,512,512]{2,1,0:T(8,128)(2,1)} %k_hbm.1, bf16[2,512,512]{2,1,0:T(8,128)(2,1)} %v_hbm.1, f32[2,512]{1,0:T(2,128)} %bitcast.15, ...), custom_call_target="tpu_custom_call" | custom-call | tf_op jit(solution)/shard_map/pallas_call | solution.py:478
  107.3 0.0 copy-start.2
  107.3 0.0 copy-start.1
  107.3 2.6 %copy.20 = bf16[2,512,640]{2,1,0:T(8,128)(2,1)} copy(bf16[2,512,640]{2,1,0:T(8,128)(2,1)} %get-tuple-element.16) | data formatting | bytes 2621440
  109.8 0.0 copy-done.2
  109.8 0.0 copy-start
  109.9 0.8 copy.21
  110.6 0.0 copy-done.1
  110.6 0.8 copy.22
  111.4 0.0 copy-done
  111.4 0.8 copy.23
Async XLA Ops:
  107.3 2.6 %copy-start.2 = (bf16[512,512]{1,0:T(8,128)(2,1)S(1)}, bf16[512,512]{1,0:T(8,128)(2,1)}, u32[]{:S(2)}) copy-start(bf16[512,512]{1,0:T(8,128)(2,1)} %get-tuple-element.9) | copy-start | bytes 1572868
  107.3 3.4 %copy-start.1 = (bf16[512,512]{1,0:T(8,128)(2,1)S(1)}, bf16[512,512]{1,0:T(8,128)(2,1)}, u32[]{:S(2)}) copy-start(bf16[512,512]{1,0:T(8,128)(2,1)} %get-tuple-element.10) | copy-start | bytes 1572868
  109.8 1.6 %copy-start = (bf16[512,512]{1,0:T(8,128)(2,1)S(1)}, bf16[512,512]{1,0:T(8,128)(2,1)}, u32[]{:S(2)}) copy-start(bf16[512,512]{1,0:T(8,128)(2,1)} %get-tuple-element.11) | copy-start | bytes 1572868

commit v4 on v3

--- a/solution.py
+++ b/solution.py
@@ -428,8 +428,8 @@
     interleave(
         sum_gradients(0),
         [
-            lambda: (send_far(0, (2, 3)), hidden(0, 0)),
-            lambda: (hidden(0, 1), fast_out()),
+            lambda: (send_far(0, (2,)), hidden(0, 0)),
+            lambda: (send_far(0, (3,)), hidden(0, 1), fast_out()),
             nothing,
             nothing,
             lambda: attend(0, 0),

time: 112 us -> 111 us (level)
    pallas_call x1, Pallas kernels: 105 us -> 104 us  [local(): pl.pallas_call(functools.partial(kernel, zs, ys), out_shape=(jax.ShapeDty...]
where the time goes in v4:
time: 111 us
  Pallas kernels  104 us (94%)
  local copies, waits for them, and re-layouts  6.24 us (6%)
    pallas_call x1, Pallas kernels, local(): pl.pallas_call(functools.partial(kernel, zs, ys), out_shape=(jax.ShapeDty...  104 us
    unnamed x11, local copies, waits for them, and re-layouts  6.24 us

profile of v4, /device:TPU:1, one launch (start us, length us, event | category | flops | bytes accessed | tf_op | source)
XLA Modules:
  0.0 111.0 jit_solution(8127726474263341475)
XLA Ops:
  0.6 1.3 %copy.15 = f32[2,1,512]{2,0,1:T(2,128)} copy(f32[2,1,512]{2,1,0:T(1,128)} %param.12) | data formatting | bytes 8192
  1.9 104.1 %shard_map.120 = (bf16[2,512,640]{2,1,0:T(8,128)(2,1)}, bf16[512,512]{1,0:T(8,128)(2,1)}, bf16[512,512]{1,0:T(8,128)(2,1)}, bf16[512,512]{1,0:T(8,128)(2,1)}) custom-call(bf16[2,512,512]{2,1,0:T(8,128)(2,1)} %q_hbm.1, bf16[2,512,512]{2,1,0:T(8,128)(2,1)} %k_hbm.1, bf16[2,512,512]{2,1,0:T(8,128)(2,1)} %v_hbm.1, f32[2,512]{1,0:T(2,128)} %bitcast.15, ...), custom_call_target="tpu_custom_call" | custom-call | tf_op jit(solution)/shard_map/pallas_call | solution.py:478
  106.0 0.0 copy-start.2
  106.0 0.0 copy-start.1
  106.0 2.6 %copy.20 = bf16[2,512,640]{2,1,0:T(8,128)(2,1)} copy(bf16[2,512,640]{2,1,0:T(8,128)(2,1)} %get-tuple-element.16) | data formatting | bytes 2621440
  108.6 0.0 copy-done.2
  108.6 0.0 copy-start
  108.6 0.8 copy.21
  109.4 0.0 copy-done.1
  109.4 0.8 copy.22
  110.2 0.0 copy-done
  110.2 0.8 copy.23
Async XLA Ops:
  106.0 2.6 %copy-start.2 = (bf16[512,512]{1,0:T(8,128)(2,1)S(1)}, bf16[512,512]{1,0:T(8,128)(2,1)}, u32[]{:S(2)}) copy-start(bf16[512,512]{1,0:T(8,128)(2,1)} %get-tuple-element.9) | copy-start | bytes 1572868
  106.0 3.4 %copy-start.1 = (bf16[512,512]{1,0:T(8,128)(2,1)S(1)}, bf16[512,512]{1,0:T(8,128)(2,1)}, u32[]{:S(2)}) copy-start(bf16[512,512]{1,0:T(8,128)(2,1)} %get-tuple-element.10) | copy-start | bytes 1572868
  108.6 1.6 %copy-start = (bf16[512,512]{1,0:T(8,128)(2,1)S(1)}, bf16[512,512]{1,0:T(8,128)(2,1)}, u32[]{:S(2)}) copy-start(bf16[512,512]{1,0:T(8,128)(2,1)} %get-tuple-element.11) | copy-start | bytes 1572868
